TPU v7x, 32 devices: a whole 2x2x4 slice. The times are simulated.
32 devices in a mesh: mem: 16 (over z, x, core), dec: 2 (over y).
Axes of the slice: x: 2, y: 2, z: 4, core: 2. Of those that a mesh axis runs over, the one named last changes fastest.
Arguments:
- question_states: bfloat16 [16, 8, 4096], P('mem', None, 'dec'), may hold values from -6 to 6
- passage_cache: bfloat16 [64, 64, 4096], P('mem', None, 'dec'), may hold values from -6 to 6
- norm_gain: float32 [4096], replicated, may hold values from 0.1 to 1.9
- enc_wq: bfloat16 [4096, 2048], P('mem', 'dec'), may hold values from -0.09375 to 0.09375
- enc_wk: bfloat16 [4096, 2048], P('mem', 'dec'), may hold values from -0.09375 to 0.09375
- enc_wv: bfloat16 [4096, 2048], P('mem', 'dec'), may hold values from -0.09375 to 0.09375
- enc_wo: bfloat16 [2048, 4096], P('dec', 'mem'), may hold values from -0.125 to 0.125
- dec_wk: bfloat16 [4096, 2048], P('dec'), may hold values from -0.09375 to 0.09375
- dec_wv: bfloat16 [4096, 2048], P('dec'), may hold values from -0.09375 to 0.09375
- dec_queries: bfloat16 [16, 8, 2048], P('mem', None, 'dec'), may hold values from -6 to 6
- passage_ids: int32 [16, 2], replicated, may hold values from 0 to 63, as said below
- location: int32 [64], replicated, may hold values from 0 to 63, as said below
- question_lengths: int32 [16], replicated, may hold values from 1 to 8
Outputs:
- decoder_context: bfloat16 [16, 8, 2048], P('mem', None, 'dec')
Inputs may be any that keep to these rules, and one draw needn't show every extreme that they name: `passage_ids`: the requests whose passage lies in cache rows s * 4 to (s + 1) * 4 - 1 number at most 3 for every s, and exactly 3 for some s; a question's passages need not differ. A permutation: passage p's states are row location[p] of passage_cache.
All inputs are finite; a program needn't handle non-finite values.
Results may differ from a plain program's by a relative error of at most 0.04.
Values may be sent and summed in bfloat16 or wider, within the bound.
No kernel may reach another device: no remote copies, remote signals or barrier semaphores. Data moves between devices by JAX's collectives and lax.ppermute only.
A program may use at most 128 MiB of HBM per device.

v0:
```python
import jax
import jax.numpy as jnp
from jax import lax
from jax.sharding import PartitionSpec as P

HEAD_DIM = 64
CAP = 3


NORM_EPSILON = 1e-06


def body(
    question_states,
    passage_cache,
    norm_gain,
    enc_wq,
    enc_wk,
    enc_wv,
    enc_wo,
    dec_wk,
    dec_wv,
    dec_queries,
    passage_ids,
    location,
    question_lengths,
):
    mem_count = lax.axis_size("mem")
    mem_index = lax.axis_index("mem")
    pass_count = passage_ids.shape[1]
    request_total = mem_count * pass_count
    stored_count = passage_cache.shape[0]
    question_rows = question_states.shape[1]
    pair_rows = question_rows + passage_cache.shape[1]
    answer_rows = dec_queries.shape[1]
    heads_here = dec_queries.shape[2] // HEAD_DIM
    score_scale = HEAD_DIM ** (-0.5)
    cache_row = jnp.take(location, passage_ids.reshape(-1))
    owner_index = cache_row // stored_count
    cache_slot = cache_row % stored_count
    served = (owner_index == mem_index).astype(jnp.int32)
    served_rank = jnp.cumsum(served) - 1
    taken_mask = (served[None, :] == 1) & (served_rank[None, :] == jnp.arange(CAP)[:, None])
    filled = jnp.any(taken_mask, axis=1)
    request = jnp.sum(jnp.where(taken_mask, jnp.arange(request_total)[None, :], 0), axis=1)
    asking = request // pass_count
    pick_index = request % pass_count
    local_slot = jnp.sum(jnp.where(taken_mask, cache_slot[None, :], 0), axis=1)
    every_question, every_query = (
        lax.all_gather(question_states, "mem", axis=0, tiled=True),
        lax.all_gather(dec_queries, "mem", axis=0, tiled=True),
    )
    asked_states = every_question[asking]
    asked_queries = every_query[asking]
    asked_passages = passage_cache[local_slot]
    local_rows = jnp.concatenate([asked_states, asked_passages], axis=1)
    full_rows = lax.all_gather(local_rows, "dec", axis=2, tiled=True)
    model_width = full_rows.shape[2]
    squares = jnp.mean(jnp.square(full_rows.astype(jnp.float32)), axis=2, keepdims=True)
    normed = (full_rows.astype(jnp.float32) * lax.rsqrt(squares + NORM_EPSILON) * norm_gain).astype(
        jnp.bfloat16
    )
    row_total = CAP * pair_rows
    flattened = normed.reshape(row_total, model_width)
    local_width = enc_wq.shape[1]
    pieces = (
        lax.all_gather(enc_wq, "mem", axis=0, tiled=True),
        lax.all_gather(enc_wk, "mem", axis=0, tiled=True),
        lax.all_gather(enc_wv, "mem", axis=0, tiled=True),
    )
    query_sums, key_sums, value_sums = tuple(
        (
            jnp.dot(flattened, weight_piece, preferred_element_type=jnp.float32)
            for weight_piece in pieces
        )
    )
    shape_four = (CAP, pair_rows, heads_here, HEAD_DIM)
    queries = query_sums.astype(jnp.bfloat16).reshape(shape_four)
    enc_keys = key_sums.astype(jnp.bfloat16).reshape(shape_four)
    enc_values = value_sums.astype(jnp.bfloat16).reshape(shape_four)
    lengths_here = question_lengths[asking]
    positions = jnp.arange(pair_rows)
    live_keys = (
        (positions[None, :] >= question_rows) | (positions[None, :] < lengths_here[:, None])
    ).astype(jnp.float32)
    scores = (
        jnp.einsum("cihe,cjhe->chij", queries, enc_keys, preferred_element_type=jnp.float32)
        * score_scale
    )
    weights = jnp.exp(scores) * live_keys[:, None, None, :]
    probabilities = (weights / jnp.sum(weights, axis=3, keepdims=True)).astype(jnp.bfloat16)
    context = (
        jnp.einsum("chij,cjhe->cihe", probabilities, enc_values, preferred_element_type=jnp.float32)
        .astype(jnp.bfloat16)
        .reshape(row_total, local_width)
    )
    partial_out = jnp.dot(
        context,
        lax.all_gather(enc_wo, "mem", axis=1, tiled=True),
        preferred_element_type=jnp.float32,
    )
    attended = lax.psum_scatter(
        partial_out.astype(jnp.bfloat16), "dec", scatter_dimension=1, tiled=True
    ).astype(jnp.float32)
    encoded = (local_rows.reshape(row_total, -1).astype(jnp.float32) + attended).astype(
        jnp.bfloat16
    )
    key_part = jnp.dot(encoded, dec_wk, preferred_element_type=jnp.float32)
    value_part = jnp.dot(encoded, dec_wv, preferred_element_type=jnp.float32)
    key_share, value_share = (
        lax.psum_scatter(
            key_part.astype(jnp.bfloat16), "dec", scatter_dimension=1, tiled=True
        ).astype(jnp.float32),
        lax.psum_scatter(
            value_part.astype(jnp.bfloat16), "dec", scatter_dimension=1, tiled=True
        ).astype(jnp.float32),
    )
    dec_keys = key_share.astype(jnp.bfloat16).reshape(shape_four)
    dec_values = value_share.astype(jnp.bfloat16).reshape(shape_four)
    asked = asked_queries.reshape(CAP, answer_rows, heads_here, HEAD_DIM)
    cross_scores = (
        jnp.einsum("cahe,cjhe->chaj", asked, dec_keys, preferred_element_type=jnp.float32)
        * score_scale
    )
    keep_keys = live_keys * filled.astype(jnp.float32)[:, None]
    cross_weight = jnp.exp(cross_scores) * keep_keys[:, None, None, :]
    numerators = jnp.einsum(
        "chaj,cjhe->cahe",
        cross_weight.astype(jnp.bfloat16),
        dec_values,
        preferred_element_type=jnp.float32,
    ).reshape(CAP, -1)
    denominators = jnp.transpose(jnp.sum(cross_weight, axis=3), (0, 2, 1)).reshape(CAP, -1)
    target_pairs = (
        (asking[:, None, None] == jnp.arange(mem_count)[None, :, None])
        & (pick_index[:, None, None] == jnp.arange(pass_count)[None, None, :])
        & filled[:, None, None]
    ).astype(jnp.float32)
    back_numer = jnp.einsum(
        "cqk,cx->qkx", target_pairs, numerators, precision=lax.Precision.HIGHEST
    )
    back_denom = jnp.einsum(
        "cqk,cx->qkx", target_pairs, denominators, precision=lax.Precision.HIGHEST
    )
    got_numer, got_denom = (
        lax.all_to_all(
            back_numer.astype(jnp.bfloat16), "mem", split_axis=0, concat_axis=0, tiled=True
        ).astype(back_numer.dtype),
        lax.all_to_all(
            back_denom.astype(jnp.bfloat16), "mem", split_axis=0, concat_axis=0, tiled=True
        ).astype(back_denom.dtype),
    )
    numerator_sum = jnp.sum(got_numer, axis=(0, 1))
    denominator_sum = jnp.sum(got_denom, axis=(0, 1))
    answer = (
        numerator_sum.reshape(answer_rows, heads_here, HEAD_DIM)
        / denominator_sum.reshape(answer_rows, heads_here)[:, :, None]
    )
    return answer.reshape(1, answer_rows, heads_here * HEAD_DIM).astype(jnp.bfloat16)


def solution(mesh):
    in_specs = (
        P("mem", None, "dec"),
        P("mem", None, "dec"),
        P(),
        P("mem", "dec"),
        P("mem", "dec"),
        P("mem", "dec"),
        P("dec", "mem"),
        P("dec", None),
        P("dec", None),
        P("mem", None, "dec"),
        P(),
        P(),
        P(),
    )
    out_specs = P("mem", None, "dec")
    return jax.shard_map(body, mesh=mesh, in_specs=in_specs, out_specs=out_specs, check_vma=False)
```

profile of v0, /device:TPU:0, one launch (start us, length us, event | category | flops | bytes accessed | tf_op | source)
XLA Modules:
  0.0 491.5 jit_solution(17326156538032678646)
XLA Ops:
  6.5 0.8 copy.77
  7.5 0.1 reshape.503
  7.5 0.1 fusion.20
  7.7 1.4 gather_fusion
  9.0 0.1 copy.82
  9.2 0.1 add_reduce_fusion
  9.4 0.1 fusion.35
  9.5 0.1 select_reduce_fusion
  9.7 24.8 %all_gather.21 = bf16[16,8,2048]{2,1,0:T(8,128)(2,1)S(1)} all-gather(bf16[1,8,2048]{2,1,0:T(8,128)(2,1)} %param.13), channel_id=1, replica_groups=mesh['mem'=16,'dec'=2] {'mem'}, dimensions={0}, use_global_device_ids=true | all-gather | bytes 557056 | tf_op jit(solution)/shard_map/all_gather | solution.py:50
  34.5 0.6 gather_fusion.1
  35.1 0.6 gather_fusion.2
  35.8 0.9 copy-done.4
  36.8 0.7 all-gather.10.cloned.1.call-update
  37.5 0.7 all-gather.12.cloned.1.call-update
  38.2 0.5 all-gather.8.cloned.1.call-update
  38.8 0.5 all-gather.14.cloned.1.call-update
  39.4 0.6 gather_fusion.3
  40.1 0.1 fusion.30
  40.1 23.5 %all-gather.6.cloned.1.call-done = bf16[3,72,4096]{2,1,0:T(8,128)(2,1)} async-done(((bf16[3,72,2048]{2,1,0:T(8,128)(2,1)}), bf16[3,72,4096]{2,1,0:T(8,128)(2,1)}) %all-gather.6.cloned.1.call-update) | async-done | bytes 1769488 | tf_op jit(solution)/shard_map/all_gather | solution.py:57
  63.6 2.1 fusion
  65.7 0.5 fusion.2
  66.2 74.5 %all-gather.10.cloned.1.call-done = bf16[4096,1024]{1,0:T(8,128)(2,1)} async-done(((bf16[256,1024]{1,0:T(8,128)(2,1)}), bf16[4096,1024]{1,0:T(8,128)(2,1)}) %all-gather.10.cloned.1.call-update) | async-done | bytes 8388624 | tf_op jit(solution)/shard_map/all_gather | solution.py:67
  140.7 5.4 %convolution_convert_fusion.6 = bf16[216,1024]{1,0:T(8,128)(2,1)S(1)} fusion(bf16[216,4096]{1,0:T(8,128)(2,1)S(1)} %bitcast.46, bf16[4096,1024]{1,0:T(8,128)(2,1)} %all-gather.10.cloned.1.call-done), kind=kOutput, calls=%fused_computation.21 | convolution fusion | flops 1812160512 | bytes 10600448 | tf_op jit(solution)/shard_map/dot_general | solution.py:73
  146.1 0.5 reshape.507
  146.6 69.4 %all-gather.12.cloned.1.call-done = bf16[4096,1024]{1,0:T(8,128)(2,1)} async-done(((bf16[256,1024]{1,0:T(8,128)(2,1)}), bf16[4096,1024]{1,0:T(8,128)(2,1)}) %all-gather.12.cloned.1.call-update) | async-done | bytes 8388624 | tf_op jit(solution)/shard_map/all_gather | solution.py:68
  216.0 5.4 %convolution_convert_fusion.5 = bf16[216,1024]{1,0:T(8,128)(2,1)S(1)} fusion(bf16[216,4096]{1,0:T(8,128)(2,1)S(1)} %bitcast.47, bf16[4096,1024]{1,0:T(8,128)(2,1)} %all-gather.12.cloned.1.call-done), kind=kOutput, calls=%fused_computation.20 | convolution fusion | flops 1812160512 | bytes 10600448 | tf_op jit(solution)/shard_map/dot_general | solution.py:73
  221.4 1.5 reshape.508
  222.9 68.3 %all-gather.8.cloned.1.call-done = bf16[4096,1024]{1,0:T(8,128)(2,1)} async-done(((bf16[256,1024]{1,0:T(8,128)(2,1)}), bf16[4096,1024]{1,0:T(8,128)(2,1)}) %all-gather.8.cloned.1.call-update) | async-done | bytes 8388624 | tf_op jit(solution)/shard_map/all_gather | solution.py:69
  291.2 5.4 %convolution_convert_fusion.7 = bf16[216,1024]{1,0:T(8,128)(2,1)S(1)} fusion(bf16[216,4096]{1,0:T(8,128)(2,1)S(1)} %bitcast.48, bf16[4096,1024]{1,0:T(8,128)(2,1)} %all-gather.8.cloned.1.call-done), kind=kOutput, calls=%fused_computation.22 | convolution fusion | flops 1812160512 | bytes 10600448 | tf_op jit(solution)/shard_map/dot_general | solution.py:73
  296.6 0.5 reshape.506
  297.2 3.1 exponential_multiply_fusion
  300.3 2.7 fusion.4
  303.0 0.7 copy.87
  303.8 0.6 reshape.509
  304.4 65.2 %all-gather.14.cloned.1.call-done = bf16[1024,4096]{1,0:T(8,128)(2,1)} async-done(((bf16[1024,256]{1,0:T(8,128)(2,1)}), bf16[1024,4096]{1,0:T(8,128)(2,1)}) %all-gather.14.cloned.1.call-update) | async-done | bytes 8388624 | tf_op jit(solution)/shard_map/all_gather | solution.py:99
  369.6 6.7 %convolution_convert_fusion.1 = bf16[216,4096]{1,0:T(8,128)(2,1)} fusion(bf16[216,1024]{1,0:T(8,128)(2,1)S(1)} %reshape.509, bf16[1024,4096]{1,0:T(8,128)(2,1)} %all-gather.14.cloned.1.call-done), kind=kOutput, calls=%fused_computation.6 | convolution fusion | flops 1812824064 | bytes 10600448 | tf_op jit(solution)/shard_map/dot_general | solution.py:97
  376.3 0.2 reduce-scatter.8.cloned.1.call-start
  376.5 26.3 %reduce-scatter.4.cloned.1.call-done = bf16[216,2048]{1,0:T(8,128)(2,1)} async-done(((bf16[216,4096]{1,0:T(8,128)(2,1)}), bf16[216,2048]{1,0:T(8,128)(2,1)}) %reduce-scatter.4.cloned.1.call-update) | async-done | bytes 884752 | tf_op jit(solution)/shard_map/reduce_scatter | solution.py:102
  402.9 1.5 fusion.3
  404.3 6.3 %convolution_convert_fusion.2 = bf16[216,2048]{1,0:T(8,128)(2,1)} fusion(bf16[216,2048]{1,0:T(8,128)(2,1)S(1)} %fusion.3, bf16[2048,2048]{1,0:T(8,128)(2,1)} %param.20), kind=kOutput, calls=%fused_computation.12 | convolution fusion | flops 1812381696 | bytes 10158080 | tf_op jit(solution)/shard_map/dot_general | solution.py:108
  410.8 6.3 %convolution_convert_fusion.3 = bf16[216,2048]{1,0:T(8,128)(2,1)} fusion(bf16[216,2048]{1,0:T(8,128)(2,1)S(1)} %fusion.3, bf16[2048,2048]{1,0:T(8,128)(2,1)} %param.21), kind=kOutput, calls=%fused_computation.13 | convolution fusion | flops 1812381696 | bytes 10158080 | tf_op jit(solution)/shard_map/dot_general | solution.py:109
  417.1 22.0 %all_gather.27 = bf16[16,8,1024]{2,1,0:T(8,128)(2,1)S(1)} all-gather(bf16[1,8,1024]{2,1,0:T(8,128)(2,1)S(1)} %copy-done.7), channel_id=1, replica_groups=mesh['mem'=16,'dec'=2] {'mem'}, dimensions={0}, use_global_device_ids=true | all-gather | bytes 278528 | tf_op jit(solution)/shard_map/all_gather | solution.py:51
  439.1 0.5 gather_fusion.4
  439.7 0.1 reshape.511
  440.0 1.7 reshape.512
  441.7 0.6 fusion.37
  442.3 7.9 %reduce-scatter.6.cloned.1.call-done = bf16[216,1024]{1,0:T(8,128)(2,1)} async-done(((bf16[216,2048]{1,0:T(8,128)(2,1)}), bf16[216,1024]{1,0:T(8,128)(2,1)}) %reduce-scatter.6.cloned.1.call-update) | async-done | bytes 442384 | tf_op jit(solution)/shard_map/reduce_scatter | solution.py:114
  450.3 1.7 reshape.510
  451.9 0.4 convolution_bitcast_fusion
  452.3 0.1 reshape.557
  452.5 0.1 reshape.558
  452.6 0.3 convolution_convert_fusion.8
  452.9 0.6 copy.94
  453.5 5.6 %all-to-all-start.1 = ((bf16[16,2,128]{2,1,0:T(2,128)(2,1)}), bf16[16,2,128]{2,1,0:T(2,128)(2,1)S(1)}, u32[]{:S(2)}, u32[]{:S(2)}) async-start(bf16[16,2,128]{2,1,0:T(2,128)(2,1)} %copy.94), calls=%async_computation.4 | async-start | bytes 16384 | tf_op jit(solution)/shard_map/all_to_all | solution.py:149
  459.2 0.7 convolution_convert_fusion
  459.9 1.3 copy.92
  461.2 4.3 all-to-all-done.1
  465.5 3.6 all-to-all-start
  469.1 0.1 div.88
  469.2 0.1 div.89
  469.3 0.1 div.90
  469.4 14.1 %all-to-all-done = bf16[16,2,8192]{2,1,0:T(2,128)(2,1)S(1)} async-done(((bf16[16,2,8192]{2,1,0:T(2,128)(2,1)}), bf16[16,2,8192]{2,1,0:T(2,128)(2,1)S(1)}, u32[]{:S(2)}, u32[]{:S(2)}) %all-to-all-start) | async-done | bytes 524320 | tf_op jit(solution)/shard_map/all_to_all | solution.py:146
  483.5 0.5 convert_reduce_fusion
  484.0 0.6 divide_convert_fusion.2
  (50 shorter events, 1.0 us)
Async XLA Ops:
  6.5 28.5 %copy-start = (bf16[4,64,2048]{2,1,0:T(8,128)(2,1)S(1)}, bf16[4,64,2048]{2,1,0:T(8,128)(2,1)}, u32[]{:S(2)}) copy-start(bf16[4,64,2048]{2,1,0:T(8,128)(2,1)} %param.14) | copy-start | bytes 3145732
  6.5 57.1 %all-gather.6.cloned.1.call-start = ((), (), s32[]{:S(2)}) async-start(), calls=%async_computation.5 | async-start | bytes 2654208 | tf_op jit(solution)/shard_map/all_gather | solution.py:57
  35.7 0.9 copy-start.4
  35.8 3.7 copy-start.2
  36.7 104.0 %all-gather.10.cloned.1.call-start = ((), (), s32[]{:S(2)}) async-start(), calls=%async_computation.7 | async-start | bytes 8912896 | tf_op jit(solution)/shard_map/all_gather | solution.py:67
  37.5 178.6 %all-gather.12.cloned.1.call-start = ((), (), s32[]{:S(2)}) async-start(), calls=%async_computation.8 | async-start | bytes 8912896 | tf_op jit(solution)/shard_map/all_gather | solution.py:68
  38.2 27.5 %copy-start.6 = (f32[4096]{0:T(1024)S(1)}, f32[4096]{0:T(1024)}, u32[]{:S(2)}) copy-start(f32[4096]{0:T(1024)} %param.15) | copy-start | bytes 49156
  38.2 253.0 %all-gather.8.cloned.1.call-start = ((), (), s32[]{:S(2)}) async-start(), calls=%async_computation.6 | async-start | bytes 8912896 | tf_op jit(solution)/shard_map/all_gather | solution.py:69
  38.8 330.8 %all-gather.14.cloned.1.call-start = ((), (), s32[]{:S(2)}) async-start(), calls=%async_computation.9 | async-start | bytes 8912896 | tf_op jit(solution)/shard_map/all_gather | solution.py:99
  39.4 363.5 %reduce-scatter.4.cloned.1.call-start = ((), (), s32[]{:S(2)}) async-start(), calls=%async_computation.10 | async-start | bytes 2654208 | tf_op jit(solution)/shard_map/reduce_scatter | solution.py:102
  63.6 2.1 copy-start.3
  376.3 26.6 %copy-start.5 = (bf16[3,72,2048]{2,1,0:T(8,128)(2,1)S(1)}, bf16[3,72,2048]{2,1,0:T(8,128)(2,1)}, u32[]{:S(2)}) copy-start(bf16[3,72,2048]{2,1,0:T(8,128)(2,1)} %copy-done.4) | copy-start | bytes 2654212
  376.3 63.7 %reduce-scatter.8.cloned.1.call-start = ((), (), s32[]{:S(2)}) async-start(), calls=%async_computation.12 | async-start | bytes 1327104 | tf_op jit(solution)/shard_map/reduce_scatter | solution.py:111
  410.7 6.4 %copy-start.7 = (bf16[1,8,1024]{2,1,0:T(8,128)(2,1)S(1)}, bf16[1,8,1024]{2,1,0:T(8,128)(2,1)}, u32[]{:S(2)}) copy-start(bf16[1,8,1024]{2,1,0:T(8,128)(2,1)} %param.22) | copy-start | bytes 49156
  410.7 39.6 %reduce-scatter.6.cloned.1.call-start = ((), (), s32[]{:S(2)}) async-start(), calls=%async_computation.11 | async-start | bytes 1327104 | tf_op jit(solution)/shard_map/reduce_scatter | solution.py:114
  453.5 12.0 %all-to-all-start.1 = ((bf16[16,2,128]{2,1,0:T(2,128)(2,1)}), bf16[16,2,128]{2,1,0:T(2,128)(2,1)S(1)}, u32[]{:S(2)}, u32[]{:S(2)}) async-start(bf16[16,2,128]{2,1,0:T(2,128)(2,1)} %copy.94), calls=%async_computation.4 | async-start | bytes 16384 | tf_op jit(solution)/shard_map/all_to_all | solution.py:149
  459.2 25.4 %copy-start.1 = (bf16[4,64,2048]{2,1,0:T(8,128)(2,1)S(1)}, bf16[4,64,2048]{2,1,0:T(8,128)(2,1)}, u32[]{:S(2)}) copy-start(bf16[4,64,2048]{2,1,0:T(8,128)(2,1)} %param.14) | copy-start | bytes 3145732
  465.5 18.0 %all-to-all-start = ((bf16[16,2,8192]{2,1,0:T(2,128)(2,1)}), bf16[16,2,8192]{2,1,0:T(2,128)(2,1)S(1)}, u32[]{:S(2)}, u32[]{:S(2)}) async-start(bf16[16,2,8192]{2,1,0:T(2,128)(2,1)} %copy.92), calls=%async_computation.3 | async-start | bytes 1048576 | tf_op jit(solution)/shard_map/all_to_all | solution.py:146
Sparse Core Ops, SparseCore 0:
  36.8 26.7 all-gather.5
  65.8 74.8 all-gather.9
  142.9 73.1 all-gather.11
  218.1 73.1 all-gather.7
  293.2 76.3 all-gather.13
  376.4 26.3 reduce-scatter.3
  410.8 18.4 reduce-scatter.7
  431.7 18.5 reduce-scatter.5
where the time goes:
time: 492 us; the launch traced here: 491 us
  waiting for transfers between devices  356 us (72%)
  blocking collectives  46.8 us (10%)
  matrix products  43.3 us (9%)
  local copies, waits for them, and re-layouts  15.7 us (3%)
  between operations  13.8 us (3%)
  starting transfers between devices  9.67 us (2%)
  other arithmetic  6.08 us (1%)
    all_gather x1, waiting for transfers between devices, body(): lax.all_gather(enc_wq, 'mem', axis=0, tiled=True)  74.5 us
    all_gather x1, waiting for transfers between devices, body(): lax.all_gather(enc_wk, 'mem', axis=0, tiled=True)  69.4 us
    all_gather x1, waiting for transfers between devices, body(): lax.all_gather(enc_wv, 'mem', axis=0, tiled=True)  68.3 us
    all_gather x1, waiting for transfers between devices, body(): lax.all_gather(enc_wo, 'mem', axis=1, tiled=True)  65.2 us
    reduce_scatter x1, waiting for transfers between devices, body(): lax.psum_scatter(partial_out.astype(jnp.bfloat16), 'dec', scatter_dimensi...  26.3 us
    all_gather x1, blocking collectives, body(): lax.all_gather(question_states, 'mem', axis=0, tiled=True)  24.8 us
    all_gather x1, waiting for transfers between devices, body(): full_rows = lax.all_gather(local_rows, 'dec', axis=2, tiled=True)  23.5 us
    all_gather x1, blocking collectives, body(): lax.all_gather(dec_queries, 'mem', axis=0, tiled=True)  22 us
  transfers between devices with their start and end apart: 10, of which 9 were waited for; matrix products, arithmetic and copies ran while one was open for 8% of the time, Pallas kernels for 0%

commit v1 on v0

v1 whole, which is shorter than its diff:
```python
import jax
import jax.numpy as jnp
from jax import lax
from jax.experimental import pallas as pl
from jax.experimental.pallas import tpu as pltpu
from jax.sharding import PartitionSpec as P

HEAD_DIM = 64
CAP = 3


NORM_EPSILON = 1e-06


def split_mem(mem_count):
    line_count = 1 << (mem_count.bit_length() // 2)
    return line_count, mem_count // line_count


def bits_of(inner_count):
    return [1 << k for k in range(inner_count.bit_length() - 1)]


def swap_mem(value, mask, mem_count):
    return lax.ppermute(value, "mem", [(i, i ^ mask) for i in range(mem_count)])


def over_dec(value, dec_index, dec_count):
    parts = [value]
    for step in range(1, dec_count):
        parts.append(
            lax.ppermute(value, "dec", [(i, (i - step) % dec_count) for i in range(dec_count)])
        )
    twice = jnp.stack(parts + parts)
    ordered = lax.dynamic_slice_in_dim(twice, (dec_count - dec_index) % dec_count, dec_count, 0)
    return jnp.moveaxis(ordered, 0, -2).reshape(value.shape[:-1] + (dec_count * value.shape[-1],))


def over_dec_halves(value, upper, dec_index, dec_count):
    if dec_count == 2:
        other = lax.ppermute(value, "dec", [(0, 1), (1, 0)])
        same = upper == (dec_index == 1)
        return jnp.where(same, value, other), jnp.where(same, other, value)
    whole = over_dec(value, dec_index, dec_count)
    half = whole.shape[1] // 2
    low, high = whole[:, :half], whole[:, half:]
    return jnp.where(upper, high, low), jnp.where(upper, low, high)


def dec_sum(value, dec_count):
    total = value
    for step in range(1, dec_count):
        total = total + lax.ppermute(
            value, "dec", [(i, (i + step) % dec_count) for i in range(dec_count)]
        )
    return total


def shift_line(value, step, first, last, inner_count):
    pairs = [
        (at * inner_count + b, (at + step) * inner_count + b)
        for at in range(first, last)
        for b in range(inner_count)
    ]
    return lax.ppermute(value, "mem", pairs)


def gather_line(value, axis, line_index, line_count, inner_count):
    upward, downward = [value], [value]
    for step in range(1, line_count):
        upward.append(shift_line(upward[-1], 1, step - 1, line_count - 1, inner_count))
        downward.append(shift_line(downward[-1], -1, 1, line_count - step + 1, inner_count))
    ordered = jnp.concatenate(upward[:0:-1] + [value] + downward[1:], axis=axis)
    size = value.shape[axis]
    return lax.dynamic_slice_in_dim(
        ordered, (line_count - 1 - line_index) * size, line_count * size, axis
    )


def after(value, *earlier):
    return lax.optimization_barrier((value, *earlier))[0]


def along(sent, pairs, inner_count):
    return lax.ppermute(
        sent,
        "mem",
        [(a * inner_count + b, c * inner_count + b) for a, c in pairs for b in range(inner_count)],
    )


def beside(value, inner_count):
    return along(value, [(0, 1), (1, 0), (2, 3), (3, 2)], inner_count)


def far_half(near, line_index, inner_count):
    across = along(near, [(1, 2), (2, 1)], inner_count)
    outward = along(across, [(1, 0), (2, 3)], inner_count)
    middle = (line_index == 1) | (line_index == 2)
    return jnp.where(middle, across, outward)


def attention_kernel(heads, lives_ref, query_ref, key_ref, value_ref, out_ref):
    slots, rows, _ = query_ref.shape
    lanes = 2 * HEAD_DIM
    lane = lax.broadcasted_iota(jnp.int32, (rows, lanes), 1)
    key_at = lax.broadcasted_iota(jnp.int32, (rows, rows), 1)
    first = lane < HEAD_DIM
    for slot in range(slots):
        live = (key_at < lives_ref[0, slot]) | (key_at >= lives_ref[1, slot])
        for pair in range(heads // 2):
            span = slice(pair * lanes, (pair + 1) * lanes)
            query = query_ref[slot, :, span] * HEAD_DIM ** (-0.5)
            key = key_ref[slot, :, span].astype(jnp.bfloat16)
            value = value_ref[slot, :, span].astype(jnp.bfloat16)
            outs = []
            for chosen in (first, ~first):
                scores = lax.dot_general(
                    jnp.where(chosen, query, 0.0).astype(jnp.bfloat16),
                    key,
                    (((1,), (1,)), ((), ())),
                    preferred_element_type=jnp.float32,
                )
                weights = jnp.where(live, jnp.exp(scores), 0.0)
                total = jnp.sum(weights, axis=1, keepdims=True)
                probabilities = (weights / total).astype(jnp.bfloat16)
                outs.append(jnp.dot(probabilities, value, preferred_element_type=jnp.float32))
            out_ref[slot, :, span] = jnp.where(first, outs[0], outs[1])


def attend(lives, queries, keys, values):
    heads = queries.shape[2] // HEAD_DIM
    return pl.pallas_call(
        lambda *refs: attention_kernel(heads, *refs),
        out_shape=jax.ShapeDtypeStruct(queries.shape, jnp.float32),
        in_specs=[pl.BlockSpec(memory_space=pltpu.SMEM)]
        + [pl.BlockSpec(memory_space=pltpu.VMEM)] * 3,
        out_specs=pl.BlockSpec(memory_space=pltpu.VMEM),
        compiler_params=pltpu.CompilerParams(vmem_limit_bytes=24 * 1024 * 1024),
        cost_estimate=pl.CostEstimate(
            flops=4 * queries.shape[0] * queries.shape[1] ** 2 * queries.shape[2],
            bytes_accessed=16 * queries.size,
            transcendentals=queries.shape[0] * queries.shape[1] ** 2 * heads,
        ),
    )(lives, queries, keys, values)


def body(
    question_states,
    passage_cache,
    norm_gain,
    enc_wq,
    enc_wk,
    enc_wv,
    enc_wo,
    dec_wk,
    dec_wv,
    dec_queries,
    passage_ids,
    location,
    question_lengths,
):
    mem_count = lax.axis_size("mem")
    mem_index = lax.axis_index("mem")
    dec_count = lax.axis_size("dec")
    dec_index = lax.axis_index("dec")
    line_count, inner_count = split_mem(mem_count)
    line_index, inner_index = mem_index // inner_count, mem_index % inner_count
    pass_count = passage_ids.shape[1]
    request_total = mem_count * pass_count
    stored_count = passage_cache.shape[0]
    question_rows = question_states.shape[1]
    pair_rows = question_rows + passage_cache.shape[1]
    row_total = CAP * pair_rows
    answer_rows = dec_queries.shape[1]
    local_features = question_states.shape[2]
    heads_width = dec_queries.shape[2]
    heads_here = heads_width // HEAD_DIM
    score_scale = HEAD_DIM ** (-0.5)
    model_width = local_features * dec_count

    cache_row = jnp.take(location, passage_ids.reshape(-1))
    owner_index = cache_row // stored_count
    cache_slot = cache_row % stored_count
    served = (owner_index == mem_index).astype(jnp.int32)
    served_rank = jnp.cumsum(served) - 1
    taken_mask = (served[None, :] == 1) & (served_rank[None, :] == jnp.arange(CAP)[:, None])
    filled = jnp.any(taken_mask, axis=1)
    request = jnp.sum(jnp.where(taken_mask, jnp.arange(request_total)[None, :], 0), axis=1)
    asking = request // pass_count
    local_slot = jnp.sum(jnp.where(taken_mask, cache_slot[None, :], 0), axis=1)

    relay = line_count == 4
    if relay:
        query_beside = beside(enc_wq, inner_count)
    sent = jnp.concatenate([question_states, dec_queries], axis=2)
    sent = jnp.concatenate(
        [sent] + [swap_mem(sent, mask, mem_count) for mask in range(1, inner_count)], axis=0
    )
    came = [
        swap_mem(sent, mask, mem_count) for mask in range(inner_count, mem_count, inner_count)
    ]
    if relay:
        both_weights = after(jnp.concatenate([enc_wk, enc_wv], axis=0), came[0])
        both_beside = beside(both_weights, inner_count)
    sent = jnp.concatenate([sent] + came, axis=0)
    asked = sent[asking ^ mem_index]
    asked_states = asked[:, :, :local_features]
    asked_queries = over_dec(asked[:, :, local_features:], dec_index, dec_count)

    asked_passages = passage_cache[local_slot]
    local_rows = jnp.concatenate([asked_states, asked_passages], axis=1).reshape(row_total, -1)
    wide_rows = local_rows.astype(jnp.float32)
    squares = jnp.sum(jnp.square(wide_rows), axis=1, keepdims=True)
    row_scale = lax.rsqrt(dec_sum(squares, dec_count) / model_width + NORM_EPSILON)
    local_gain = lax.dynamic_slice_in_dim(norm_gain, dec_index * local_features, local_features)
    gained = (wide_rows * local_gain).astype(jnp.bfloat16)

    block = model_width // mem_count
    here = line_count // dec_count
    by_inner = gained.reshape(row_total, here, inner_count, block)

    def features_for(mask):
        picked = lax.dynamic_index_in_dim(by_inner, inner_index ^ mask, 2, keepdims=False)
        return picked.reshape(row_total, here * block)

    masks = [0]
    for bit in reversed(bits_of(inner_count)):
        masks = masks + [mask + bit for mask in masks]
    plane_rows = jnp.concatenate(
        [features_for(0)] + [swap_mem(features_for(k), k, mem_count) for k in masks[1:]], axis=0
    )
    upper = line_index >= line_count // 2
    near_rows, far_rows = over_dec_halves(plane_rows, upper, dec_index, dec_count)

    def halves(weight, weight_beside):
        if not relay:
            whole = gather_line(weight, 0, line_index, line_count, inner_count)
            half = whole.shape[0] // 2
            low, high = whole[:half], whole[half:]
            return jnp.where(upper, high, low), jnp.where(upper, low, high)
        near = jnp.where(
            line_index % 2 == 1,
            jnp.concatenate([weight_beside, weight], axis=0),
            jnp.concatenate([weight, weight_beside], axis=0),
        )
        return near, far_half(near, line_index, inner_count)

    def project(weight, weight_beside):
        near_weight, far_weight = halves(weight, weight_beside)

        def rows_sum(low, high):
            return jnp.dot(
                near_rows[low:high], near_weight, preferred_element_type=jnp.float32
            ) + jnp.dot(far_rows[low:high], far_weight, preferred_element_type=jnp.float32)

        rows = near_rows.shape[0]
        total = None
        for bit in bits_of(inner_count):
            rows //= 2
            if total is None:
                given, kept = rows_sum(rows, 2 * rows), rows_sum(0, rows)
            else:
                given, kept = total[rows:], total[:rows]
            total = kept + swap_mem(given.astype(jnp.bfloat16), bit, mem_count).astype(
                jnp.float32
            )
        return (total * row_scale).reshape(CAP, pair_rows, -1)

    block_rows = enc_wk.shape[0]
    besides = (
        (query_beside, both_beside[:block_rows], both_beside[block_rows:]) if relay else [None] * 3
    )
    queries, enc_keys, enc_values = (
        project(weight, near) for weight, near in zip((enc_wq, enc_wk, enc_wv), besides)
    )
    lengths_here = question_lengths[asking]
    positions = jnp.arange(pair_rows)
    live_keys = (
        (positions[None, :] >= question_rows) | (positions[None, :] < lengths_here[:, None])
    ).astype(jnp.float32)
    lives = jnp.stack([lengths_here, jnp.full_like(lengths_here, question_rows)])
    context = (
        attend(lives, queries, enc_keys, enc_values)
        .reshape(row_total, heads_width)
        .astype(jnp.bfloat16)
    )
    out_weight = lax.all_gather(after(enc_wo, plane_rows), "mem", axis=1, tiled=True)

    def out_columns(first, size):
        return jnp.dot(
            context,
            lax.dynamic_slice_in_dim(out_weight, first, size, 1),
            preferred_element_type=jnp.float32,
        )

    chunk = local_features // 2
    received = []
    for part in range(2):
        came = 0.0
        for step in range(1, dec_count):
            goal = (dec_index + step) % dec_count
            given = out_columns(goal * local_features + part * chunk, chunk).astype(jnp.bfloat16)
            came = came + lax.ppermute(
                given, "dec", [(i, (i + step) % dec_count) for i in range(dec_count)]
            ).astype(jnp.float32)
        received.append(came)
    kept = wide_rows + out_columns(dec_index * local_features, local_features)
    encoded = (kept + jnp.concatenate(received, axis=1)).astype(jnp.bfloat16)

    head_total = asked_queries.shape[2] // HEAD_DIM
    own_head = (
        jnp.arange(head_total * HEAD_DIM)[None, :] // HEAD_DIM == jnp.arange(head_total)[:, None]
    )
    spread = jnp.where(own_head[None, :, None, :], asked_queries[:, None], 0)
    wide_queries = lax.dot_general(
        spread.reshape(-1, head_total * HEAD_DIM),
        dec_wk,
        (((1,), (1,)), ((), ())),
        preferred_element_type=jnp.float32,
    ).astype(jnp.bfloat16)
    slot_rows = encoded.reshape(CAP, pair_rows, local_features)
    cross_scores = dec_sum(
        jnp.einsum(
            "cmf,cjf->cmj",
            wide_queries.reshape(CAP, head_total * answer_rows, local_features),
            slot_rows,
            preferred_element_type=jnp.float32,
        ),
        dec_count,
    )
    keep_keys = live_keys * filled.astype(jnp.float32)[:, None]
    cross_weight = jnp.exp(cross_scores * score_scale) * keep_keys[:, None, :]
    dec_values = jnp.dot(encoded, dec_wv, preferred_element_type=jnp.float32).astype(jnp.bfloat16)
    products = jnp.einsum(
        "cmj,cjv->cmv",
        cross_weight.astype(jnp.bfloat16),
        dec_values.reshape(CAP, pair_rows, -1),
        preferred_element_type=jnp.float32,
    ).reshape(CAP, head_total, answer_rows, -1)
    sums = jnp.sum(jnp.where(own_head[None, :, None, :], products, 0.0), axis=1)
    blocks = sums.reshape(CAP, answer_rows, dec_count, heads_width)

    def block_of(index):
        return lax.dynamic_index_in_dim(blocks, index, 2, keepdims=False)

    numerators = block_of(dec_index)
    for step in range(1, dec_count):
        numerators = numerators + lax.ppermute(
            block_of((dec_index + step) % dec_count).astype(jnp.bfloat16),
            "dec",
            [(i, (i + step) % dec_count) for i in range(dec_count)],
        ).astype(jnp.float32)
    every_denominator = jnp.sum(cross_weight, axis=2).reshape(CAP, head_total, answer_rows)
    denominators = lax.dynamic_slice_in_dim(
        every_denominator, dec_index * heads_here, heads_here, 1
    )
    both = jnp.concatenate(
        [
            numerators.reshape(CAP, -1),
            jnp.transpose(denominators, (0, 2, 1)).reshape(CAP, -1),
        ],
        axis=1,
    )
    targets = (
        (asking[:, None] == jnp.arange(mem_count)[None, :]) & filled[:, None]
    ).astype(jnp.float32)
    back = sum(targets[c][:, None] * both[c][None, :] for c in range(CAP))
    got = lax.all_to_all(
        back.astype(jnp.bfloat16), "mem", split_axis=0, concat_axis=0, tiled=True
    ).astype(jnp.float32)
    got_sum = jnp.sum(got, axis=0)
    numerator_sum = got_sum[: answer_rows * heads_width]
    denominator_sum = got_sum[answer_rows * heads_width :]
    answer = (
        numerator_sum.reshape(answer_rows, heads_here, HEAD_DIM)
        / denominator_sum.reshape(answer_rows, heads_here)[:, :, None]
    )
    return answer.reshape(1, answer_rows, heads_width).astype(jnp.bfloat16)


def solution(mesh):
    in_specs = (
        P("mem", None, "dec"),
        P("mem", None, "dec"),
        P(),
        P("mem", "dec"),
        P("mem", "dec"),
        P("mem", "dec"),
        P("dec", "mem"),
        P("dec", None),
        P("dec", None),
        P("mem", None, "dec"),
        P(),
        P(),
        P(),
    )
    out_specs = P("mem", None, "dec")
    return jax.shard_map(body, mesh=mesh, in_specs=in_specs, out_specs=out_specs, check_vma=False)
```

time: 492 us -> 316 us (0.64)
  waiting for transfers between devices: 356 us -> 190 us
  blocking collectives: 46.8 us -> 12.9 us
  starting transfers between devices: 9.67 us -> 32.7 us
  matrix products: 43.3 us -> 30.5 us
  other arithmetic: 6.08 us -> 15.7 us
    all_gather x5 -> x1, waiting for transfers between devices: 301 us -> 0.02 us  [body(): lax.all_gather(after(enc_wo, plane_rows), 'mem', axis=1, tiled=True)]
    ppermute x0 -> x30, waiting for transfers between devices: none -> 190 us  [the longest x8 133 us: along(): lax.ppermute(sent, 'mem', [(a * inner_count + b, c * inner_count + b) for...]
    all_gather x2 -> x0, blocking collectives: 46.8 us -> none  [the longest x1 24.8 us: body(): lax.all_gather(question_states, 'mem', axis=0, tiled=True)]
    reduce_scatter x3 -> x0, waiting for transfers between devices: 34.3 us -> none  [the longest x1 26.3 us: body(): lax.psum_scatter(partial_out.astype(jnp.bfloat16), 'dec', scatter_dimensi...]
    ppermute x0 -> x30, starting transfers between devices: none -> 32.7 us  [the longest x15 13.9 us: swap_mem(): return lax.ppermute(value, 'mem', [(i, i ^ mask) for i in range(mem_count)])]
    all_to_all x2 -> x0, waiting for transfers between devices: 18.4 us -> none  [the longest x1 14.1 us: body(): lax.all_to_all(back_numer.astype(jnp.bfloat16), 'mem', split_axis=0, conc...]
    all_to_all x0 -> x1, blocking collectives: none -> 12.9 us  [body(): lax.all_to_all(back.astype(jnp.bfloat16), 'mem', split_axis=0, concat_axi...]
    dot_general x12 -> x19, matrix products: 43.3 us -> 30.5 us  [the longest x1 9.26 us: body(): lax.dot_general(spread.reshape(-1, head_total * HEAD_DIM), dec_wk, (((1,)...]
  transfers between devices with their start and end apart: 10 -> 31, of which waited for: 9 -> 15; matrix products, arithmetic and copies ran while one was open for 8% -> 15% of each run, Pallas kernels for 0% -> 1%
where the time goes in v1:
time: 316 us
  waiting for transfers between devices  190 us (60%)
  starting transfers between devices  32.7 us (10%)
  matrix products  30.5 us (10%)
  local copies, waits for them, and re-layouts  17.4 us (6%)
  other arithmetic  15.7 us (5%)
  between operations  14.3 us (5%)
  blocking collectives  12.9 us (4%)
    ppermute x8, waiting for transfers between devices, along(): lax.ppermute(sent, 'mem', [(a * inner_count + b, c * inner_count + b) for...  133 us
    ppermute x15, waiting for transfers between devices, swap_mem(): return lax.ppermute(value, 'mem', [(i, i ^ mask) for i in range(mem_count)])  43.8 us
    ppermute x15, starting transfers between devices, swap_mem(): return lax.ppermute(value, 'mem', [(i, i ^ mask) for i in range(mem_count)])  13.9 us
    all_to_all x1, blocking collectives, body(): lax.all_to_all(back.astype(jnp.bfloat16), 'mem', split_axis=0, concat_axi...  12.9 us
    ppermute x8, starting transfers between devices, along(): lax.ppermute(sent, 'mem', [(a * inner_count + b, c * inner_count + b) for...  10.6 us
    dot_general x1, matrix products, body(): lax.dot_general(spread.reshape(-1, head_total * HEAD_DIM), dec_wk, (((1,)...  9.26 us
    ppermute x2, waiting for transfers between devices, body(): lax.ppermute(given, 'dec', [(i, (i + step) % dec_count) for i in range(de...  7.52 us
  transfers between devices with their start and end apart: 31, of which 15 were waited for; matrix products, arithmetic and copies ran while one was open for 15% of the time, Pallas kernels for 1%

profile of v1, /device:TPU:0, one launch (start us, length us, event | category | flops | bytes accessed | tf_op | source)
XLA Modules:
  0.0 315.5 jit_solution(15092606957749695202)
XLA Ops:
  6.5 0.9 constant_dynamic-update-slice_fusion.1
  7.4 0.7 constant_dynamic-update-slice_fusion
  8.1 2.4 collective-permute-start.2
  11.2 0.8 copy.59
  12.2 1.4 gather_fusion
  14.7 0.7 dynamic_slice.39
  16.2 1.9 collective-permute-start.3
  18.1 2.6 collective-permute-start.4
  20.7 6.4 %collective-permute-done.3 = bf16[4,8,3072]{2,1,0:T(8,128)(2,1)S(1)} collective-permute-done((bf16[4,8,3072]{2,1,0:T(8,128)(2,1)S(1)}, bf16[4,8,3072]{2,1,0:T(8,128)(2,1)S(1)}, u32[]{:S(2)}, u32[]{:S(2)}) %collective-permute-start.3) | collective-permute-done | bytes 196640 | tf_op jit(solution)/shard_map/ppermute | solution.py:25
  27.1 8.0 %collective-permute-done.4 = bf16[4,8,3072]{2,1,0:T(8,128)(2,1)S(1)} collective-permute-done((bf16[4,8,3072]{2,1,0:T(8,128)(2,1)S(1)}, bf16[4,8,3072]{2,1,0:T(8,128)(2,1)S(1)}, u32[]{:S(2)}, u32[]{:S(2)}) %collective-permute-start.4) | collective-permute-done | bytes 196640 | tf_op jit(solution)/shard_map/ppermute | solution.py:25
  35.8 0.7 copy-done.10
  37.3 1.2 reshape.714
  38.5 0.9 fusion.10
  40.1 1.6 collective-permute-start.7
  41.9 0.7 collective-permute-start.9
  42.5 0.7 constant_dynamic-update-slice_fusion.13
  43.2 4.0 %collective-permute-done.7 = bf16[216,512]{1,0:T(8,128)(2,1)S(1)} collective-permute-done((bf16[216,512]{1,0:T(8,128)(2,1)S(1)}, bf16[216,512]{1,0:T(8,128)(2,1)S(1)}, u32[]{:S(2)}, u32[]{:S(2)}) %collective-permute-start.7) | collective-permute-done | bytes 221216 | tf_op jit(solution)/shard_map/ppermute | solution.py:25
  47.3 0.7 constant_dynamic-update-slice_fusion.12
  48.0 0.7 constant_dynamic-update-slice_fusion.11
  48.7 1.2 collective-permute-done.9
  49.9 0.7 constant_dynamic-update-slice_fusion.10
  50.6 4.1 %collective-permute-start.11 = (bf16[256,1024]{1,0:T(8,128)(2,1)}, bf16[256,1024]{1,0:T(8,128)(2,1)}, u32[]{:S(2)}, u32[]{:S(2)}) collective-permute-start(bf16[256,1024]{1,0:T(8,128)(2,1)} %param.16), channel_id=1, source_target_pairs={{0,8},{2,10},{4,12},{6,14},{8,0},{10,2},{12,4},{14,6},{16,24},{18,... | collective-permute-start | bytes 1572872 | tf_op jit(solution)/shard_map/ppermute | solution.py:85
  55.4 2.2 pad_maximum_fusion.1
  58.3 1.5 collective-permute-start.16
  59.9 0.8 fusion.77
  61.2 1.5 collective-permute-start.10
  62.7 2.5 collective-permute-done.6
  65.3 7.4 %collective-permute-done.11 = bf16[256,1024]{1,0:T(8,128)(2,1)} collective-permute-done((bf16[256,1024]{1,0:T(8,128)(2,1)}, bf16[256,1024]{1,0:T(8,128)(2,1)}, u32[]{:S(2)}, u32[]{:S(2)}) %collective-permute-start.11) | collective-permute-done | bytes 524320 | tf_op jit(solution)/shard_map/ppermute | solution.py:85
  72.7 2.3 maximum_select_fusion
  75.0 0.9 collective-permute-start.12
  75.9 33.0 %collective-permute-done.17 = bf16[512,1024]{1,0:T(8,128)(2,1)} collective-permute-done((bf16[512,1024]{1,0:T(8,128)(2,1)}, bf16[512,1024]{1,0:T(8,128)(2,1)}, u32[]{:S(2)}, u32[]{:S(2)}) %collective-permute-start.17) | collective-permute-done | bytes 1048608 | tf_op jit(solution)/shard_map/ppermute | solution.py:85
  108.8 1.3 fusion.76
  110.6 0.7 collective-permute-start.22
  111.9 0.7 collective-permute-start.18
  112.6 1.3 broadcast_select_fusion.4
  115.2 1.3 collective-permute-start.13
  117.7 1.3 collective-permute-start.23
  119.7 1.5 collective-permute-start.19
  121.8 48.2 %collective-permute-done.13 = bf16[512,1024]{1,0:T(8,128)(2,1)S(1)} collective-permute-done((bf16[512,1024]{1,0:T(8,128)(2,1)S(1)}, bf16[512,1024]{1,0:T(8,128)(2,1)S(1)}, u32[]{:S(2)}, u32[]{:S(2)}) %collective-permute-start.13) | collective-permute-done | bytes 1048608 | tf_op jit(solution)/shard_map/ppermute | solution.py:85
  171.4 22.8 %collective-permute-done.23 = bf16[512,1024]{1,0:T(8,128)(2,1)S(1)} collective-permute-done((bf16[512,1024]{1,0:T(8,128)(2,1)S(1)}, bf16[512,1024]{1,0:T(8,128)(2,1)S(1)}, u32[]{:S(2)}, u32[]{:S(2)}) %collective-permute-start.23) | collective-permute-done | bytes 1048608 | tf_op jit(solution)/shard_map/ppermute | solution.py:85
  194.8 21.8 %collective-permute-done.19 = bf16[512,1024]{1,0:T(8,128)(2,1)S(1)} collective-permute-done((bf16[512,1024]{1,0:T(8,128)(2,1)S(1)}, bf16[512,1024]{1,0:T(8,128)(2,1)S(1)}, u32[]{:S(2)}, u32[]{:S(2)}) %collective-permute-start.19) | collective-permute-done | bytes 1048608 | tf_op jit(solution)/shard_map/ppermute | solution.py:85
  216.6 0.7 add_convert_fusion.2
  219.3 1.7 collective-permute-start.15
  222.8 1.7 collective-permute-start.21
  224.5 2.3 broadcast_select_fusion
  226.8 5.6 %collective-permute-done.15 = bf16[216,1024]{1,0:T(8,128)(2,1)S(1)} collective-permute-done((bf16[216,1024]{1,0:T(8,128)(2,1)S(1)}, bf16[216,1024]{1,0:T(8,128)(2,1)S(1)}, u32[]{:S(2)}, u32[]{:S(2)}) %collective-permute-start.15) | collective-permute-done | bytes 442400 | tf_op jit(solution)/shard_map/ppermute | solution.py:25
  232.3 9.5 %collective-permute-done.25 = bf16[216,1024]{1,0:T(8,128)(2,1)S(1)} collective-permute-done((bf16[216,1024]{1,0:T(8,128)(2,1)S(1)}, bf16[216,1024]{1,0:T(8,128)(2,1)S(1)}, u32[]{:S(2)}, u32[]{:S(2)}) %collective-permute-start.25) | collective-permute-done | bytes 442400 | tf_op jit(solution)/shard_map/ppermute | solution.py:25
  241.8 9.1 %collective-permute-done.21 = bf16[216,1024]{1,0:T(8,128)(2,1)S(1)} collective-permute-done((bf16[216,1024]{1,0:T(8,128)(2,1)S(1)}, bf16[216,1024]{1,0:T(8,128)(2,1)S(1)}, u32[]{:S(2)}, u32[]{:S(2)}) %collective-permute-start.21) | collective-permute-done | bytes 442400 | tf_op jit(solution)/shard_map/ppermute | solution.py:25
  250.9 0.7 fusion.19
  251.6 2.1 shard_map.127
  253.8 2.4 fusion.14
  256.2 1.6 collective-permute-start.27
  257.8 2.4 fusion.11
  260.7 9.3 %convolution_convert_fusion = bf16[768,2048]{1,0:T(8,128)(2,1)S(1)} fusion(bf16[768,2048]{1,0:T(8,128)(2,1)S(1)} %bitcast.103, bf16[2048,2048]{1,0:T(8,128)(2,1)} %param.20), kind=kOutput, calls=%fused_computation.8 | convolution fusion | flops 6444023808 | bytes 14680064 | tf_op jit(solution)/shard_map/dot_general | solution.py:316
  270.0 7.5 %collective-permute-done.26 = bf16[216,1024]{1,0:T(8,128)(2,1)S(1)} collective-permute-done((bf16[216,1024]{1,0:T(8,128)(2,1)S(1)}, bf16[216,1024]{1,0:T(8,128)(2,1)S(1)}, u32[]{:S(2)}, u32[]{:S(2)}) %collective-permute-start.26) | collective-permute-done | bytes 442400 | tf_op jit(solution)/shard_map/ppermute | solution.py:304
  277.5 1.2 add_convert_fusion
  278.8 1.1 fusion.78
  279.9 1.6 collective-permute-start.28
  281.5 5.4 %convolution_convert_fusion.1 = bf16[216,2048]{1,0:T(8,128)(2,1)S(1)} fusion(bf16[216,2048]{1,0:T(8,128)(2,1)S(1)} %add_convert_fusion, bf16[2048,2048]{1,0:T(8,128)(2,1)} %param.21), kind=kOutput, calls=%fused_computation.11 | convolution fusion | flops 1812381696 | bytes 10158080 | tf_op jit(solution)/shard_map/dot_general | solution.py:334
  286.9 1.2 fusion
  288.1 0.8 collective-permute-start.29
  289.3 3.0 collective-permute-done.29
  293.4 0.8 reduce.12
  294.4 12.9 %all_to_all.6 = bf16[16,2,4160]{2,1,0:T(2,128)(2,1)S(1)} all-to-all(bf16[16,2,4160]{2,1,0:T(2,128)(2,1)S(1)} %reshape.753), channel_id=1, replica_groups=mesh['mem'=16,'dec'=2] {'mem'}, dimensions={0} | all-to-all | bytes 532480 | tf_op jit(solution)/shard_map/all_to_all | solution.py:369
  (151 shorter events, 21.2 us)
Async XLA Ops:
  6.5 8.9 %copy-start = (bf16[4,64,2048]{2,1,0:T(8,128)(2,1)S(1)}, bf16[4,64,2048]{2,1,0:T(8,128)(2,1)}, u32[]{:S(2)}) copy-start(bf16[4,64,2048]{2,1,0:T(8,128)(2,1)} %param.14) | copy-start | bytes 3145732
  6.5 247.2 %all-gather.2.cloned.1.call-start = ((), (), s32[]{:S(2)}) async-start(), calls=%async_computation.1 | async-start | bytes 8912896 | tf_op jit(solution)/shard_map/all_gather | solution.py:288
  8.1 8.0 %collective-permute-start.2 = (bf16[1,8,3072]{2,1,0:T(8,128)(2,1)S(1)}, bf16[1,8,3072]{2,1,0:T(8,128)(2,1)S(1)}, u32[]{:S(2)}, u32[]{:S(2)}) collective-permute-start(bf16[1,8,3072]{2,1,0:T(8,128)(2,1)S(1)} %get-tuple-element.30), channel_id=1, source_target_pairs={{0,6},{2,4},{4,2},{6,0},{8,14},{10,12},{12,10},{14,8},{16,22},{18,... | collective-permute-start | bytes 147464 | tf_op jit(solution)/shard_map/ppermute | solution.py:25
  10.5 5.6 %collective-permute-start.1 = (bf16[1,8,3072]{2,1,0:T(8,128)(2,1)S(1)}, bf16[1,8,3072]{2,1,0:T(8,128)(2,1)S(1)}, u32[]{:S(2)}, u32[]{:S(2)}) collective-permute-start(bf16[1,8,3072]{2,1,0:T(8,128)(2,1)S(1)} %get-tuple-element.30), channel_id=1, source_target_pairs={{0,4},{2,6},{4,0},{6,2},{8,12},{10,14},{12,8},{14,10},{16,20},{18,... | collective-permute-start | bytes 147464 | tf_op jit(solution)/shard_map/ppermute | solution.py:25
  11.1 5.0 %collective-permute-start = (bf16[1,8,3072]{2,1,0:T(8,128)(2,1)S(1)}, bf16[1,8,3072]{2,1,0:T(8,128)(2,1)S(1)}, u32[]{:S(2)}, u32[]{:S(2)}) collective-permute-start(bf16[1,8,3072]{2,1,0:T(8,128)(2,1)S(1)} %get-tuple-element.30), channel_id=1, source_target_pairs={{0,2},{2,0},{4,6},{6,4},{8,10},{10,8},{12,14},{14,12},{16,18},{18,... | collective-permute-start | bytes 147464 | tf_op jit(solution)/shard_map/ppermute | solution.py:25
  14.2 0.5 copy-start.11
  16.1 20.4 %copy-start.3 = (bf16[3,64,2048]{2,1,0:T(8,128)(2,1)}, bf16[3,64,2048]{2,1,0:T(8,128)(2,1)S(1)}, u32[]{:S(2)}) copy-start(bf16[3,64,2048]{2,1,0:T(8,128)(2,1)S(1)} %gather_fusion.2) | copy-start | bytes 2359300
  16.2 10.9 %collective-permute-start.3 = (bf16[4,8,3072]{2,1,0:T(8,128)(2,1)S(1)}, bf16[4,8,3072]{2,1,0:T(8,128)(2,1)S(1)}, u32[]{:S(2)}, u32[]{:S(2)}) collective-permute-start(bf16[4,8,3072]{2,1,0:T(8,128)(2,1)S(1)} %pad_maximum_fusion.3), channel_id=1, source_target_pairs={{0,8},{2,10},{4,12},{6,14},{8,0},{10,2},{12,4},{14,6},{16,24},{18,... | collective-permute-start | bytes 589832 | tf_op jit(solution)/shard_map/ppermute | solution.py:25
  18.1 17.1 %collective-permute-start.4 = (bf16[4,8,3072]{2,1,0:T(8,128)(2,1)S(1)}, bf16[4,8,3072]{2,1,0:T(8,128)(2,1)S(1)}, u32[]{:S(2)}, u32[]{:S(2)}) collective-permute-start(bf16[4,8,3072]{2,1,0:T(8,128)(2,1)S(1)} %pad_maximum_fusion.3), channel_id=1, source_target_pairs={{0,16},{2,18},{4,20},{6,22},{8,24},{10,26},{12,28},{14,30},{16,0},... | collective-permute-start | bytes 589832 | tf_op jit(solution)/shard_map/ppermute | solution.py:25
  20.7 14.5 %collective-permute-start.5 = (bf16[4,8,3072]{2,1,0:T(8,128)(2,1)S(1)}, bf16[4,8,3072]{2,1,0:T(8,128)(2,1)S(1)}, u32[]{:S(2)}, u32[]{:S(2)}) collective-permute-start(bf16[4,8,3072]{2,1,0:T(8,128)(2,1)S(1)} %pad_maximum_fusion.3), channel_id=1, source_target_pairs={{0,24},{2,26},{4,28},{6,30},{8,16},{10,18},{12,20},{14,22},{16,8},... | collective-permute-start | bytes 589832 | tf_op jit(solution)/shard_map/ppermute | solution.py:25
  35.8 0.7 copy-start.10
  36.5 0.6 copy-start.8
  40.1 7.2 %collective-permute-start.7 = (bf16[216,512]{1,0:T(8,128)(2,1)S(1)}, bf16[216,512]{1,0:T(8,128)(2,1)S(1)}, u32[]{:S(2)}, u32[]{:S(2)}) collective-permute-start(bf16[216,512]{1,0:T(8,128)(2,1)S(1)} %bitcast.112), channel_id=1, source_target_pairs={{0,4},{2,6},{4,0},{6,2},{8,12},{10,14},{12,8},{14,10},{16,20},{18,... | collective-permute-start | bytes 663560 | tf_op jit(solution)/shard_map/ppermute | solution.py:25
  41.7 13.0 %copy-start.2 = (s32[16]{0:T(128)S(1)}, s32[16]{0:T(128)}, u32[]{:S(2)}) copy-start(s32[16]{0:T(128)} %param.25) | copy-start | bytes 196
  41.7 13.7 %copy-start.6 = (bf16[256,1024]{1,0:T(8,128)(2,1)S(1)}, bf16[256,1024]{1,0:T(8,128)(2,1)}, u32[]{:S(2)}) copy-start(bf16[256,1024]{1,0:T(8,128)(2,1)} %param.18) | copy-start | bytes 1572868
  41.7 6.2 %collective-permute-start.8 = (bf16[216,512]{1,0:T(8,128)(2,1)S(1)}, bf16[216,512]{1,0:T(8,128)(2,1)S(1)}, u32[]{:S(2)}, u32[]{:S(2)}) collective-permute-start(bf16[216,512]{1,0:T(8,128)(2,1)S(1)} %bitcast.113), channel_id=1, source_target_pairs={{0,2},{2,0},{4,6},{6,4},{8,10},{10,8},{12,14},{14,12},{16,18},{18,... | collective-permute-start | bytes 663560 | tf_op jit(solution)/shard_map/ppermute | solution.py:25
  41.9 8.0 %collective-permute-start.9 = (bf16[216,512]{1,0:T(8,128)(2,1)S(1)}, bf16[216,512]{1,0:T(8,128)(2,1)S(1)}, u32[]{:S(2)}, u32[]{:S(2)}) collective-permute-start(bf16[216,512]{1,0:T(8,128)(2,1)S(1)} %bitcast.114), channel_id=1, source_target_pairs={{0,6},{2,4},{4,2},{6,0},{8,14},{10,12},{12,10},{14,8},{16,22},{18,... | collective-permute-start | bytes 663560 | tf_op jit(solution)/shard_map/ppermute | solution.py:25
  48.7 8.9 %copy-start.12 = (s32[3]{0:T(128)S(1)}, s32[3]{0:T(128)}, u32[]{:S(2)}) copy-start(s32[3]{0:T(128)} %copy-done.11) | copy-start | bytes 40
  50.5 7.4 %copy-start.4 = (bf16[3,64,2048]{2,1,0:T(8,128)(2,1)S(1)}, bf16[3,64,2048]{2,1,0:T(8,128)(2,1)}, u32[]{:S(2)}) copy-start(bf16[3,64,2048]{2,1,0:T(8,128)(2,1)} %copy-done.3) | copy-start | bytes 2359300
  50.5 7.4 %copy-start.9 = (bf16[3,8,2048]{2,1,0:T(8,128)(2,1)S(1)}, bf16[3,8,2048]{2,1,0:T(8,128)(2,1)}, u32[]{:S(2)}) copy-start(bf16[3,8,2048]{2,1,0:T(8,128)(2,1)} %copy-done.8) | copy-start | bytes 294916
  50.6 22.1 %collective-permute-start.11 = (bf16[256,1024]{1,0:T(8,128)(2,1)}, bf16[256,1024]{1,0:T(8,128)(2,1)}, u32[]{:S(2)}, u32[]{:S(2)}) collective-permute-start(bf16[256,1024]{1,0:T(8,128)(2,1)} %param.16), channel_id=1, source_target_pairs={{0,8},{2,10},{4,12},{6,14},{8,0},{10,2},{12,4},{14,6},{16,24},{18,... | collective-permute-start | bytes 1572872 | tf_op jit(solution)/shard_map/ppermute | solution.py:85
  57.7 51.1 %collective-permute-start.17 = (bf16[512,1024]{1,0:T(8,128)(2,1)}, bf16[512,1024]{1,0:T(8,128)(2,1)}, u32[]{:S(2)}, u32[]{:S(2)}) collective-permute-start(bf16[512,1024]{1,0:T(8,128)(2,1)} %pad_maximum_fusion.1), channel_id=1, source_target_pairs={{0,8},{2,10},{4,12},{6,14},{8,0},{10,2},{12,4},{14,6},{16,24},{18,... | collective-permute-start | bytes 3145736 | tf_op jit(solution)/shard_map/ppermute | solution.py:85
  58.3 4.4 %collective-permute-start.16 = (f32[216,1]{0,1:T(1,128)S(1)}, f32[216,1]{0,1:T(1,128)S(1)}, u32[]{:S(2)}, u32[]{:S(2)}) collective-permute-start(f32[216,1]{0,1:T(1,128)S(1)} %broadcast_in_dim.93), channel_id=1, source_target_pairs={{0,1},{1,0},{2,3},{3,2},{4,5},{5,4},{6,7},{7,6},{8,9},{9,8},{10,11... | collective-permute-start | bytes 2600 | tf_op jit(solution)/shard_map/ppermute | solution.py:53
  60.7 4.6 %collective-permute-start.6 = (bf16[3,8,1024]{2,1,0:T(8,128)(2,1)S(1)}, bf16[3,8,1024]{2,1,0:T(8,128)(2,1)S(1)}, u32[]{:S(2)}, u32[]{:S(2)}) collective-permute-start(bf16[3,8,1024]{2,1,0:T(8,128)(2,1)S(1)} %get-tuple-element.26), channel_id=1, source_target_pairs={{0,1},{1,0},{2,3},{3,2},{4,5},{5,4},{6,7},{7,6},{8,9},{9,8},{10,11... | collective-permute-start | bytes 147464 | tf_op jit(solution)/shard_map/ppermute | solution.py:32
  61.2 51.4 %collective-permute-start.10 = (bf16[864,512]{1,0:T(8,128)(2,1)}, bf16[864,512]{1,0:T(8,128)(2,1)S(1)}, u32[]{:S(2)}, u32[]{:S(2)}) collective-permute-start(bf16[864,512]{1,0:T(8,128)(2,1)} %constant_dynamic-update-slice_fusion.10), channel_id=1, source_target_pairs={{0,1},{1,0},{2,3},{3,2},{4,5},{5,4},{6,7},{7,6},{8,9},{9,8},{10,11... | collective-permute-start | bytes 2654216 | tf_op jit(solution)/shard_map/ppermute | solution.py:41
  75.0 36.4 %copy-start.7 = (bf16[256,1024]{1,0:T(8,128)(2,1)S(1)}, bf16[256,1024]{1,0:T(8,128)(2,1)}, u32[]{:S(2)}) copy-start(bf16[256,1024]{1,0:T(8,128)(2,1)} %param.17) | copy-start | bytes 1572868
  75.0 40.1 %collective-permute-start.12 = (bf16[512,1024]{1,0:T(8,128)(2,1)S(1)}, bf16[512,1024]{1,0:T(8,128)(2,1)S(1)}, u32[]{:S(2)}, u32[]{:S(2)}) collective-permute-start(bf16[512,1024]{1,0:T(8,128)(2,1)S(1)} %maximum_select_fusion), channel_id=1, source_target_pairs={{8,16},{10,18},{12,20},{14,22},{16,8},{18,10},{20,12},{22,14},{9,1... | collective-permute-start | bytes 3145736 | tf_op jit(solution)/shard_map/ppermute | solution.py:85
  110.6 7.1 %collective-permute-start.22 = (bf16[512,1024]{1,0:T(8,128)(2,1)S(1)}, bf16[512,1024]{1,0:T(8,128)(2,1)S(1)}, u32[]{:S(2)}, u32[]{:S(2)}) collective-permute-start(bf16[512,1024]{1,0:T(8,128)(2,1)S(1)} %fusion.18), channel_id=1, source_target_pairs={{8,16},{10,18},{12,20},{14,22},{16,8},{18,10},{20,12},{22,14},{9,1... | collective-permute-start | bytes 3145736 | tf_op jit(solution)/shard_map/ppermute | solution.py:85
  111.9 7.8 %collective-permute-start.18 = (bf16[512,1024]{1,0:T(8,128)(2,1)S(1)}, bf16[512,1024]{1,0:T(8,128)(2,1)S(1)}, u32[]{:S(2)}, u32[]{:S(2)}) collective-permute-start(bf16[512,1024]{1,0:T(8,128)(2,1)S(1)} %fusion.17), channel_id=1, source_target_pairs={{8,16},{10,18},{12,20},{14,22},{16,8},{18,10},{20,12},{22,14},{9,1... | collective-permute-start | bytes 3145736 | tf_op jit(solution)/shard_map/ppermute | solution.py:85
  115.2 54.8 %collective-permute-start.13 = (bf16[512,1024]{1,0:T(8,128)(2,1)S(1)}, bf16[512,1024]{1,0:T(8,128)(2,1)S(1)}, u32[]{:S(2)}, u32[]{:S(2)}) collective-permute-start(bf16[512,1024]{1,0:T(8,128)(2,1)S(1)} %collective-permute-done.12), channel_id=1, source_target_pairs={{8,0},{10,2},{12,4},{14,6},{16,24},{18,26},{20,28},{22,30},{9,1},{... | collective-permute-start | bytes 3145736 | tf_op jit(solution)/shard_map/ppermute | solution.py:85
  117.7 76.4 %collective-permute-start.23 = (bf16[512,1024]{1,0:T(8,128)(2,1)S(1)}, bf16[512,1024]{1,0:T(8,128)(2,1)S(1)}, u32[]{:S(2)}, u32[]{:S(2)}) collective-permute-start(bf16[512,1024]{1,0:T(8,128)(2,1)S(1)} %collective-permute-done.22), channel_id=1, source_target_pairs={{8,0},{10,2},{12,4},{14,6},{16,24},{18,26},{20,28},{22,30},{9,1},{... | collective-permute-start | bytes 3145736 | tf_op jit(solution)/shard_map/ppermute | solution.py:85
  119.7 96.9 %collective-permute-start.19 = (bf16[512,1024]{1,0:T(8,128)(2,1)S(1)}, bf16[512,1024]{1,0:T(8,128)(2,1)S(1)}, u32[]{:S(2)}, u32[]{:S(2)}) collective-permute-start(bf16[512,1024]{1,0:T(8,128)(2,1)S(1)} %collective-permute-done.18), channel_id=1, source_target_pairs={{8,0},{10,2},{12,4},{14,6},{16,24},{18,26},{20,28},{22,30},{9,1},{... | collective-permute-start | bytes 3145736 | tf_op jit(solution)/shard_map/ppermute | solution.py:85
  170.6 48.0 %collective-permute-start.14 = (bf16[432,1024]{1,0:T(8,128)(2,1)S(1)}, bf16[432,1024]{1,0:T(8,128)(2,1)S(1)}, u32[]{:S(2)}, u32[]{:S(2)}) collective-permute-start(bf16[432,1024]{1,0:T(8,128)(2,1)S(1)} %add_convert_fusion.3), channel_id=1, source_target_pairs={{0,2},{2,0},{4,6},{6,4},{8,10},{10,8},{12,14},{14,12},{16,18},{18,... | collective-permute-start | bytes 2654216 | tf_op jit(solution)/shard_map/ppermute | solution.py:25
  194.8 26.2 %collective-permute-start.24 = (bf16[432,1024]{1,0:T(8,128)(2,1)S(1)}, bf16[432,1024]{1,0:T(8,128)(2,1)S(1)}, u32[]{:S(2)}, u32[]{:S(2)}) collective-permute-start(bf16[432,1024]{1,0:T(8,128)(2,1)S(1)} %add_convert_fusion.1), channel_id=1, source_target_pairs={{0,2},{2,0},{4,6},{6,4},{8,10},{10,8},{12,14},{14,12},{16,18},{18,... | collective-permute-start | bytes 2654216 | tf_op jit(solution)/shard_map/ppermute | solution.py:25
  217.2 4.9 %collective-permute-start.20 = (bf16[432,1024]{1,0:T(8,128)(2,1)S(1)}, bf16[432,1024]{1,0:T(8,128)(2,1)S(1)}, u32[]{:S(2)}, u32[]{:S(2)}) collective-permute-start(bf16[432,1024]{1,0:T(8,128)(2,1)S(1)} %add_convert_fusion.2), channel_id=1, source_target_pairs={{0,2},{2,0},{4,6},{6,4},{8,10},{10,8},{12,14},{14,12},{16,18},{18,... | collective-permute-start | bytes 2654216 | tf_op jit(solution)/shard_map/ppermute | solution.py:25
  219.3 13.0 %collective-permute-start.15 = (bf16[216,1024]{1,0:T(8,128)(2,1)S(1)}, bf16[216,1024]{1,0:T(8,128)(2,1)S(1)}, u32[]{:S(2)}, u32[]{:S(2)}) collective-permute-start(bf16[216,1024]{1,0:T(8,128)(2,1)S(1)} %slice.188), channel_id=1, source_target_pairs={{0,4},{2,6},{4,0},{6,2},{8,12},{10,14},{12,8},{14,10},{16,20},{18,... | collective-permute-start | bytes 1327112 | tf_op jit(solution)/shard_map/ppermute | solution.py:25
  221.7 20.2 %collective-permute-start.25 = (bf16[216,1024]{1,0:T(8,128)(2,1)S(1)}, bf16[216,1024]{1,0:T(8,128)(2,1)S(1)}, u32[]{:S(2)}, u32[]{:S(2)}) collective-permute-start(bf16[216,1024]{1,0:T(8,128)(2,1)S(1)} %slice.186), channel_id=1, source_target_pairs={{0,4},{2,6},{4,0},{6,2},{8,12},{10,14},{12,8},{14,10},{16,20},{18,... | collective-permute-start | bytes 1327112 | tf_op jit(solution)/shard_map/ppermute | solution.py:25
  222.8 28.1 %collective-permute-start.21 = (bf16[216,1024]{1,0:T(8,128)(2,1)S(1)}, bf16[216,1024]{1,0:T(8,128)(2,1)S(1)}, u32[]{:S(2)}, u32[]{:S(2)}) collective-permute-start(bf16[216,1024]{1,0:T(8,128)(2,1)S(1)} %slice.187), channel_id=1, source_target_pairs={{0,4},{2,6},{4,0},{6,2},{8,12},{10,14},{12,8},{14,10},{16,20},{18,... | collective-permute-start | bytes 1327112 | tf_op jit(solution)/shard_map/ppermute | solution.py:25
  253.8 6.9 %copy-start.5 = (bf16[3,32,8,2048]{3,2,1,0:T(8,128)(2,1)S(1)}, bf16[3,32,8,2048]{3,2,1,0:T(8,128)(2,1)}, u32[]{:S(2)}) copy-start(bf16[3,32,8,2048]{3,2,1,0:T(8,128)(2,1)} %broadcast_select_fusion) | copy-start | bytes 9437188
  256.2 13.8 %collective-permute-start.27 = (bf16[216,1024]{1,0:T(8,128)(2,1)S(1)}, bf16[216,1024]{1,0:T(8,128)(2,1)S(1)}, u32[]{:S(2)}, u32[]{:S(2)}) collective-permute-start(bf16[216,1024]{1,0:T(8,128)(2,1)S(1)} %fusion.14), channel_id=1, source_target_pairs={{0,1},{1,0},{2,3},{3,2},{4,5},{5,4},{6,7},{7,6},{8,9},{9,8},{10,11... | collective-permute-start | bytes 1327112 | tf_op jit(solution)/shard_map/ppermute | solution.py:304
  257.8 19.7 %slice-start = ((s8[8388608]{0:T(1024)(128)(4,1)}), s8[4194304]{0:T(1024)(128)(4,1)S(1)}, s32[]{:S(2)}) async-start(s8[8388608]{0:T(1024)(128)(4,1)} %bitcast.97), calls=%async_computation.2 | async-start | bytes 8388608
  260.1 17.4 %collective-permute-start.26 = (bf16[216,1024]{1,0:T(8,128)(2,1)S(1)}, bf16[216,1024]{1,0:T(8,128)(2,1)S(1)}, u32[]{:S(2)}, u32[]{:S(2)}) collective-permute-start(bf16[216,1024]{1,0:T(8,128)(2,1)S(1)} %fusion.11), channel_id=1, source_target_pairs={{0,1},{1,0},{2,3},{3,2},{4,5},{5,4},{6,7},{7,6},{8,9},{9,8},{10,11... | collective-permute-start | bytes 1327112 | tf_op jit(solution)/shard_map/ppermute | solution.py:304
  260.7 16.8 %slice-start.1 = ((s8[8388608]{0:T(1024)(128)(4,1)}), s8[4194304]{0:T(1024)(128)(4,1)S(1)}, s32[]{:S(2)}) async-start(s8[8388608]{0:T(1024)(128)(4,1)} %bitcast.97), calls=%async_computation.3 | async-start | bytes 8388608
  279.9 7.0 %collective-permute-start.28 = (f32[3,256,72]{1,2,0:T(8,128)S(1)}, f32[3,256,72]{1,2,0:T(8,128)S(1)}, u32[]{:S(2)}, u32[]{:S(2)}) collective-permute-start(f32[3,256,72]{1,2,0:T(8,128)S(1)} %fusion.78), channel_id=1, source_target_pairs={{0,1},{1,0},{2,3},{3,2},{4,5},{5,4},{6,7},{7,6},{8,9},{9,8},{10,11... | collective-permute-start | bytes 663560 | tf_op jit(solution)/shard_map/ppermute | solution.py:53
  288.1 4.2 %collective-permute-start.29 = (bf16[3,8,1024]{2,1,0:T(8,128)(2,1)S(1)}, bf16[3,8,1024]{2,1,0:T(8,128)(2,1)S(1)}, u32[]{:S(2)}, u32[]{:S(2)}) collective-permute-start(bf16[3,8,1024]{2,1,0:T(8,128)(2,1)S(1)} %fusion.50), channel_id=1, source_target_pairs={{0,1},{1,0},{2,3},{3,2},{4,5},{5,4},{6,7},{7,6},{8,9},{9,8},{10,11... | collective-permute-start | bytes 147464 | tf_op jit(solution)/shard_map/ppermute | solution.py:349
  292.7 16.0 %copy-start.1 = (bf16[4,64,2048]{2,1,0:T(8,128)(2,1)S(1)}, bf16[4,64,2048]{2,1,0:T(8,128)(2,1)}, u32[]{:S(2)}) copy-start(bf16[4,64,2048]{2,1,0:T(8,128)(2,1)} %param.14) | copy-start | bytes 3145732
Sparse Core Ops, SparseCore 0:
  50.7 110.5 all-gather.1
